TPU v7x, 32 devices: a whole 2x2x4 slice. The times are simulated.
32 devices in a mesh: section: 4 (over y, x), frame: 4 (over z), chan: 2 (over core).
Axes of the slice: x: 2, y: 2, z: 4, core: 2. Of those that a mesh axis runs over, the one named last changes fastest.
Arguments:
- upstream: bfloat16 [512, 8, 4, 128], P('chan', None, 'frame'), may hold values from -6 to 6
- acts: bfloat16 [4, 512, 8, 4, 128], P('section', None, None, 'frame'), may hold values from -6 to 6
- weights: bfloat16 [4, 27, 512, 512], P('section', None, 'chan'), may hold values from -0.0625 to 0.0625
Outputs:
- grads: bfloat16 [4, 512, 8, 4, 128], P('section', 'chan', None, 'frame')
- weight_grads: bfloat16 [4, 27, 512, 512], P('section', None, 'chan')
All inputs are finite; a program needn't handle non-finite values.
Results may differ from a plain program's by a relative error of at most 0.03.
Values may be sent and summed in bfloat16 or wider, within the bound.
No kernel may reach another device: no remote copies, remote signals or barrier semaphores. Data moves between devices by JAX's collectives and lax.ppermute only.
A program may use at most 128 MiB of HBM per device.

v0:
```python
import jax
import jax.numpy as jnp
from jax import lax
from jax.sharding import PartitionSpec as P

BLOCK_FRAMES = 2


def with_halo(cells, sides, width):
    for axis, dim in sides:
        count = lax.axis_size(axis)
        ends = count - 1
        head = lax.slice_in_dim(cells, 0, width, axis=dim)
        tail = lax.slice_in_dim(cells, cells.shape[dim] - width, cells.shape[dim], axis=dim)
        cells = jnp.concatenate(
            [
                lax.ppermute(tail, axis, [(i, (i + 1) % count) for i in range(ends)]),
                cells,
                lax.ppermute(head, axis, [((i + 1) % count, i) for i in range(ends)]),
            ],
            axis=dim,
        )
    return cells


def shifted(value, axis, steps):
    count = lax.axis_size(axis)
    leading, last = (max(0, -steps), min(count, count - steps))
    return lax.ppermute(value, axis, [(source, source + steps) for source in range(leading, last)])


def derivative(stored):
    logistic = jax.nn.sigmoid(stored)
    return logistic * (1.0 + stored * (1.0 - logistic))


def tap_matrix(extended, frames_n, rows_n, width_n):
    pieces = []
    for t_lag in range(3):
        for r_off in (-1, 0, 1):
            for w_off in (-1, 0, 1):
                pieces.append(
                    extended[
                        :,
                        t_lag : t_lag + frames_n,
                        1 - r_off : 1 - r_off + rows_n,
                        1 - w_off : 1 - w_off + width_n,
                    ]
                )
    stacked = jnp.stack(pieces, axis=0)
    return stacked.reshape(stacked.shape[0] * stacked.shape[1], -1)


def body(upstream, acts, weights):
    group = upstream.shape[0]
    frames_all = upstream.shape[1]
    rows_n = upstream.shape[2]
    width_n = upstream.shape[3]
    channels = acts.shape[1]
    blocks_n = frames_all // BLOCK_FRAMES
    cells = BLOCK_FRAMES * rows_n * width_n
    sections = lax.axis_size("section")
    section_pos = lax.axis_index("section")
    chan_pos = lax.axis_index("chan")
    kernel_mat = weights[0].reshape(27 * group, channels)
    stored_all = acts[0]
    later = jnp.zeros((group, 2, rows_n + 2, width_n), jnp.bfloat16)
    inbound = jnp.zeros((group, BLOCK_FRAMES, rows_n, width_n), jnp.bfloat16)
    results = jnp.zeros((group, frames_all, rows_n, width_n), jnp.bfloat16)
    kernel_sum = jnp.zeros((27 * group, channels), jnp.float32)
    ticks = blocks_n + sections - 1
    for tick in range(ticks):
        order = tick - section_pos
        active = jnp.logical_and(order >= 0, order < blocks_n)
        first = (blocks_n - 1 - jnp.clip(order, 0, blocks_n - 1)) * BLOCK_FRAMES
        fresh = lax.dynamic_slice_in_dim(upstream, first, BLOCK_FRAMES, 1)
        current = jnp.where(section_pos == 0, fresh, inbound)
        framed = with_halo(current, (("frame", 2),), 1)
        extended = jnp.pad(
            jnp.concatenate([framed, later], axis=1), ((0, 0), (0, 0), (0, 0), (1, 1))
        )
        taps_mat = tap_matrix(extended, BLOCK_FRAMES, rows_n, width_n)
        stored = lax.dynamic_slice_in_dim(stored_all, first, BLOCK_FRAMES, 1)

        def busy(operand):
            return lax.dot_general(
                kernel_mat, taps_mat, (((0,), (0,)), ((), ())), preferred_element_type=jnp.float32
            )

        def resting(operand):
            return jnp.zeros((group * lax.axis_size("chan"), cells), jnp.float32)

        summed = lax.psum_scatter(
            lax.cond(active, busy, resting, 0).astype(jnp.bfloat16),
            "chan",
            scatter_dimension=0,
            tiled=True,
        ).astype(jnp.float32)
        own = lax.dynamic_slice_in_dim(stored, chan_pos * group, group, 0).astype(jnp.float32)
        updated = (
            current.astype(jnp.float32) + derivative(own) * summed.reshape(current.shape)
        ).astype(jnp.bfloat16)

        def add_kernel(total):
            values = stored.astype(jnp.float32)
            features = (
                (values * jax.nn.sigmoid(values)).astype(jnp.bfloat16).reshape(channels, cells)
            )
            return total + lax.dot_general(
                taps_mat, features, (((1,), (1,)), ((), ())), preferred_element_type=jnp.float32
            )

        def keep_kernel(total):
            return total

        kernel_sum = lax.cond(active, add_kernel, keep_kernel, kernel_sum)
        written = lax.dynamic_update_slice_in_dim(results, updated, first, 1)
        results = jnp.where(active, written, results)
        later = jnp.where(active, framed, later)
        if tick + 1 < ticks:
            inbound = shifted(updated, "section", 1)
    kernel_total = lax.psum(kernel_sum.astype(jnp.bfloat16), "frame")
    return (results[None], kernel_total.reshape(1, 27, group, channels))


def solution(mesh):
    placed = (
        P("chan", None, "frame", None),
        P("section", None, None, "frame", None),
        P("section", None, "chan", None),
    )
    return jax.shard_map(
        body,
        mesh=mesh,
        in_specs=placed,
        out_specs=(P("section", "chan", None, "frame", None), P("section", None, "chan", None)),
        check_vma=False,
    )
```

profile of v0, /device:TPU:0, one launch (start us, length us, event | category | flops | bytes accessed | tf_op | source)
XLA Modules:
  0.0 670.9 jit_solution(3497854138882908122)
XLA Ops:
  8.5 4.9 collective-permute-start
  30.5 6.1 conditional.14
  30.5 6.1 fusion.221
  37.4 6.1 reduce-scatter.8.cloned.1.call-done
  58.4 4.4 collective-permute-done.4
  74.8 6.1 conditional.15
  74.8 6.1 fusion.222
  81.7 7.9 %reduce-scatter.10.cloned.1.call-done = bf16[256,256]{1,0:T(8,128)(2,1)} async-done(((bf16[512,256]{1,0:T(8,128)(2,1)}), bf16[256,256]{1,0:T(8,128)(2,1)}) %reduce-scatter.10.cloned.1.call-update) | async-done | bytes 131088 | tf_op jit(solution)/shard_map/reduce_scatter | solution.py:93
  104.2 4.4 collective-permute-done.7
  118.4 6.0 conditional.16
  118.4 6.0 fusion.223
  125.2 8.8 %reduce-scatter.12.cloned.1.call-done = bf16[256,256]{1,0:T(8,128)(2,1)} async-done(((bf16[512,256]{1,0:T(8,128)(2,1)}), bf16[256,256]{1,0:T(8,128)(2,1)}) %reduce-scatter.12.cloned.1.call-update) | async-done | bytes 131088 | tf_op jit(solution)/shard_map/reduce_scatter | solution.py:93
  144.1 4.8 collective-permute-start.9
  164.3 6.1 conditional.17
  164.3 6.1 fusion.224
  171.3 10.7 %reduce-scatter.14.cloned.1.call-done = bf16[256,256]{1,0:T(8,128)(2,1)} async-done(((bf16[512,256]{1,0:T(8,128)(2,1)}), bf16[256,256]{1,0:T(8,128)(2,1)}) %reduce-scatter.14.cloned.1.call-update) | async-done | bytes 131088 | tf_op jit(solution)/shard_map/reduce_scatter | solution.py:93
  211.7 14.9 %reduce-scatter.16.cloned.1.call-done = bf16[256,256]{1,0:T(8,128)(2,1)} async-done(((bf16[512,256]{1,0:T(8,128)(2,1)}), bf16[256,256]{1,0:T(8,128)(2,1)}) %reduce-scatter.16.cloned.1.call-update) | async-done | bytes 131088 | tf_op jit(solution)/shard_map/reduce_scatter | solution.py:93
  241.4 4.5 collective-permute-done.16
  260.7 14.8 %reduce-scatter.18.cloned.1.call-done = bf16[256,256]{1,0:T(8,128)(2,1)} async-done(((bf16[512,256]{1,0:T(8,128)(2,1)}), bf16[256,256]{1,0:T(8,128)(2,1)}) %reduce-scatter.18.cloned.1.call-update) | async-done | bytes 131088 | tf_op jit(solution)/shard_map/reduce_scatter | solution.py:93
  305.2 10.8 %conditional.21 = (f32[6912,512]{0,1:T(8,128)}) conditional(s32[]{:T(128)} %convert_element_type.263, () %tuple.108, (bf16[1,512,8,1,128]{4,2,3,1,0:T(8,128)(2,1)S(1)}, bf16[6912,256]{1,0:T(8,128)(2,1)}, s32[]{:T(128)}) %tuple.211), branch_computations={%region_21.22_spmd, %region_22.23_spmd.clone} | conditional | flops 1812725760 | bytes 35782696 | solution.py:116
  308.9 7.1 %convolution_bitcast_fusion = f32[6912,512]{0,1:T(8,128)} fusion(bf16[6912,256]{1,0:T(8,128)(2,1)S(1)} %copy-done.7, bf16[64,8,2,128]{3,2,1,0:T(2,128)(2,1)S(1)} %bitcast.952), kind=kOutput, calls=%fused_computation | convolution fusion | flops 1811939328 | bytes 17956864 | tf_op jit(solution)/shard_map/cond/branch_1_fun/dot_general | solution.py:109
  316.0 15.6 %conditional.22 = (f32[6912,512]{0,1:T(8,128)}) conditional(s32[]{:T(128)} %convert_element_type.269, f32[6912,512]{0,1:T(8,128)} %get-tuple-element.296, (bf16[1,512,8,1,128]{4,2,3,1,0:T(8,128)(2,1)S(1)}, bf16[6912,256]{1,0:T(8,128)(2,1)}, f32[6912,512]{0,1:T(8,128)}, s32[]{:T(128)}) %tuple.199), branch_computations={%region_23.24_spmd, %region_24.25_spmd.clone} | conditional | flops 1816264704 | bytes 49938472 | solution.py:116
  319.3 12.3 %bitcast_add_fusion = f32[6912,512]{0,1:T(8,128)} fusion(f32[6912,512]{0,1:T(8,128)} %get-tuple-element.231, bf16[6912,256]{1,0:T(8,128)(2,1)S(1)} %copy-done.1, bf16[64,8,2,128]{3,2,1,0:T(2,128)(2,1)S(1)} %bitcast.947), kind=kOutput, calls=%fused_computation.6 | convolution fusion | flops 1815478272 | bytes 32112640 | tf_op jit(solution)/shard_map/cond/branch_1_fun/dot_general | solution.py:109
  331.6 15.7 %conditional.23 = (f32[6912,512]{0,1:T(8,128)}) conditional(s32[]{:T(128)} %convert_element_type.275, f32[6912,512]{0,1:T(8,128)} %get-tuple-element.297, (bf16[1,512,8,1,128]{4,2,3,1,0:T(8,128)(2,1)S(1)}, bf16[6912,256]{1,0:T(8,128)(2,1)}, f32[6912,512]{0,1:T(8,128)}, s32[]{:T(128)}) %tuple.201), branch_computations={%region_25.26_spmd, %region_26.27_spmd.clone} | conditional | flops 1816264704 | bytes 49938472 | solution.py:116
  335.1 12.3 %bitcast_add_fusion.1 = f32[6912,512]{0,1:T(8,128)} fusion(f32[6912,512]{0,1:T(8,128)} %get-tuple-element.239, bf16[6912,256]{1,0:T(8,128)(2,1)S(1)} %copy-done.2, bf16[64,8,2,128]{3,2,1,0:T(2,128)(2,1)S(1)} %bitcast.948), kind=kOutput, calls=%fused_computation.12 | convolution fusion | flops 1815478272 | bytes 32112640 | tf_op jit(solution)/shard_map/cond/branch_1_fun/dot_general | solution.py:109
  347.4 15.6 %conditional.24 = (f32[6912,512]{0,1:T(8,128)}) conditional(s32[]{:T(128)} %convert_element_type.281, f32[6912,512]{0,1:T(8,128)} %get-tuple-element.298, (bf16[1,512,8,1,128]{4,2,3,1,0:T(8,128)(2,1)S(1)}, bf16[6912,256]{1,0:T(8,128)(2,1)}, f32[6912,512]{0,1:T(8,128)}, s32[]{:T(128)}) %tuple.203), branch_computations={%region_27.28_spmd, %region_28.29_spmd.clone} | conditional | flops 1816264704 | bytes 49938472 | solution.py:116
  350.7 12.3 %bitcast_add_fusion.2 = f32[6912,512]{0,1:T(8,128)} fusion(f32[6912,512]{0,1:T(8,128)} %get-tuple-element.247, bf16[6912,256]{1,0:T(8,128)(2,1)S(1)} %copy-done.3, bf16[64,8,2,128]{3,2,1,0:T(2,128)(2,1)S(1)} %bitcast.949), kind=kOutput, calls=%fused_computation.18 | convolution fusion | flops 1815478272 | bytes 32112640 | tf_op jit(solution)/shard_map/cond/branch_1_fun/dot_general | solution.py:109
  363.2 6.5 conditional.27
  369.7 8.7 %convert_element_type.302 = bf16[6912,512]{0,1:T(8,128)(2,1)} convert(f32[6912,512]{0,1:T(8,128)} %get-tuple-element.302) | non-fusion elementwise | flops 3538944 | bytes 21233664 | tf_op jit(solution)/shard_map/convert_element_type | solution.py:122
  378.4 10.0 %copy.27 = bf16[6912,512]{1,0:T(8,128)(2,1)} copy(bf16[6912,512]{0,1:T(8,128)(2,1)} %convert_element_type.302) | data formatting | bytes 14155776 | tf_op jit(solution)/shard_map/convert_element_type | solution.py:122
  390.3 266.6 %all-reduce.10.cloned.1.call-done = bf16[1,27,256,512]{3,2,1,0:T(8,128)(2,1)} async-done(((bf16[1,27,256,512]{3,2,1,0:T(8,128)(2,1)}), bf16[1,27,256,512]{3,2,1,0:T(8,128)(2,1)}) %all-reduce.10.cloned.1.call-update) | async-done | bytes 7077904 | tf_op jit(solution)/shard_map/psum | solution.py:122
  656.9 6.7 %copy.308 = bf16[1,27,256,512]{3,2,1,0:T(8,128)(2,1)} copy(bf16[1,27,256,512]{3,2,1,0:T(8,128)(2,1)} %all-reduce.10.cloned.1.call-done) | data formatting | bytes 14155776
  (336 shorter events, 201.9 us)
Async XLA Ops:
  7.2 15.0 %copy-start.8 = (bf16[256,8,1,128]{3,1,2,0:T(8,128)(2,1)S(1)}, bf16[256,8,1,128]{3,1,2,0:T(8,128)(2,1)}, u32[]{:S(2)}) copy-start(bf16[256,8,1,128]{3,1,2,0:T(8,128)(2,1)} %param.31) | copy-start | bytes 1572868
  7.2 36.4 %reduce-scatter.8.cloned.1.call-start = ((), (), s32[]{:S(2)}) async-start(), calls=%async_computation.7 | async-start | bytes 393216 | tf_op jit(solution)/shard_map/reduce_scatter | solution.py:93
  8.5 7.7 %collective-permute-start = (bf16[256,2,1,128]{3,1,0,2:T(2,128)(2,1)S(1)}, bf16[256,2,1,128]{3,1,0,2:T(2,128)(2,1)S(1)}, u32[]{:S(2)}, u32[]{:S(2)}) collective-permute-start(bf16[256,2,1,128]{3,1,0,2:T(2,128)(2,1)S(1)} %broadcast_select_fusion.18), channel_id=1, source_target_pairs={{0,2},{2,4},{4,6},{1,3},{3,5},{5,7},{8,10},{10,12},{12,14},{9,11},... | collective-permute-start | bytes 393224 | tf_op jit(solution)/shard_map/ppermute | solution.py:17
  13.4 6.9 %collective-permute-start.1 = (bf16[256,2,1,128]{3,1,0,2:T(2,128)(2,1)S(1)}, bf16[256,2,1,128]{3,1,0,2:T(2,128)(2,1)S(1)}, u32[]{:S(2)}, u32[]{:S(2)}) collective-permute-start(bf16[256,2,1,128]{3,1,0,2:T(2,128)(2,1)S(1)} %broadcast_select_fusion.18), channel_id=1, source_target_pairs={{2,0},{4,2},{6,4},{3,1},{5,3},{7,5},{10,8},{12,10},{14,12},{11,9},... | collective-permute-start | bytes 393224 | tf_op jit(solution)/shard_map/ppermute | solution.py:19
  30.5 14.2 %copy-start = (bf16[1,512,8,1,128]{4,2,3,1,0:T(8,128)(2,1)S(1)}, bf16[1,512,8,1,128]{4,2,3,1,0:T(8,128)(2,1)}, u32[]{:S(2)}) copy-start(bf16[1,512,8,1,128]{4,2,3,1,0:T(8,128)(2,1)} %param.32) | copy-start | bytes 3145732
  37.4 52.2 %reduce-scatter.10.cloned.1.call-start = ((), (), s32[]{:S(2)}) async-start(), calls=%async_computation.8 | async-start | bytes 393216 | tf_op jit(solution)/shard_map/reduce_scatter | solution.py:93
  45.4 6.8 %collective-permute-start.2 = (bf16[256,2,1,128]{3,1,0,2:T(2,128)(2,1)S(1)}, bf16[256,2,1,128]{3,1,0,2:T(2,128)(2,1)S(1)}, u32[]{:S(2)}, u32[]{:S(2)}) collective-permute-start(bf16[256,2,1,128]{3,1,0,2:T(2,128)(2,1)S(1)} %get-tuple-element.286), channel_id=1, source_target_pairs={{0,8},{8,16},{16,24},{1,9},{9,17},{17,25},{2,10},{10,18},{18,26},{... | collective-permute-start | bytes 393224 | tf_op jit(solution)/shard_map/ppermute | solution.py:29
  52.5 5.9 collective-permute-start.3
  55.9 6.9 %collective-permute-start.4 = (bf16[256,2,1,128]{3,1,0,2:T(2,128)(2,1)S(1)}, bf16[256,2,1,128]{3,1,0,2:T(2,128)(2,1)S(1)}, u32[]{:S(2)}, u32[]{:S(2)}) collective-permute-start(bf16[256,2,1,128]{3,1,0,2:T(2,128)(2,1)S(1)} %broadcast_select_fusion.17), channel_id=1, source_target_pairs={{2,0},{4,2},{6,4},{3,1},{5,3},{7,5},{10,8},{12,10},{14,12},{11,9},... | collective-permute-start | bytes 393224 | tf_op jit(solution)/shard_map/ppermute | solution.py:19
  81.6 52.4 %reduce-scatter.12.cloned.1.call-start = ((), (), s32[]{:S(2)}) async-start(), calls=%async_computation.9 | async-start | bytes 393216 | tf_op jit(solution)/shard_map/reduce_scatter | solution.py:93
  91.3 6.8 %collective-permute-start.5 = (bf16[256,2,1,128]{3,1,0,2:T(2,128)(2,1)S(1)}, bf16[256,2,1,128]{3,1,0,2:T(2,128)(2,1)S(1)}, u32[]{:S(2)}, u32[]{:S(2)}) collective-permute-start(bf16[256,2,1,128]{3,1,0,2:T(2,128)(2,1)S(1)} %get-tuple-element.284), channel_id=1, source_target_pairs={{0,8},{8,16},{16,24},{1,9},{9,17},{17,25},{2,10},{10,18},{18,26},{... | collective-permute-start | bytes 393224 | tf_op jit(solution)/shard_map/ppermute | solution.py:29
  98.3 5.9 collective-permute-start.6
  101.8 6.9 %collective-permute-start.7 = (bf16[256,2,1,128]{3,1,0,2:T(2,128)(2,1)S(1)}, bf16[256,2,1,128]{3,1,0,2:T(2,128)(2,1)S(1)}, u32[]{:S(2)}, u32[]{:S(2)}) collective-permute-start(bf16[256,2,1,128]{3,1,0,2:T(2,128)(2,1)S(1)} %broadcast_select_fusion.16), channel_id=1, source_target_pairs={{2,0},{4,2},{6,4},{3,1},{5,3},{7,5},{10,8},{12,10},{14,12},{11,9},... | collective-permute-start | bytes 393224 | tf_op jit(solution)/shard_map/ppermute | solution.py:19
  125.2 56.7 %reduce-scatter.14.cloned.1.call-start = ((), (), s32[]{:S(2)}) async-start(), calls=%async_computation.10 | async-start | bytes 393216 | tf_op jit(solution)/shard_map/reduce_scatter | solution.py:93
  135.8 6.8 %collective-permute-start.8 = (bf16[256,2,1,128]{3,1,0,2:T(2,128)(2,1)S(1)}, bf16[256,2,1,128]{3,1,0,2:T(2,128)(2,1)S(1)}, u32[]{:S(2)}, u32[]{:S(2)}) collective-permute-start(bf16[256,2,1,128]{3,1,0,2:T(2,128)(2,1)S(1)} %get-tuple-element.280), channel_id=1, source_target_pairs={{0,8},{8,16},{16,24},{1,9},{9,17},{17,25},{2,10},{10,18},{18,26},{... | collective-permute-start | bytes 393224 | tf_op jit(solution)/shard_map/ppermute | solution.py:29
  142.8 6.9 %collective-permute-start.10 = (bf16[256,2,1,128]{3,1,0,2:T(2,128)(2,1)S(1)}, bf16[256,2,1,128]{3,1,0,2:T(2,128)(2,1)S(1)}, u32[]{:S(2)}, u32[]{:S(2)}) collective-permute-start(bf16[256,2,1,128]{3,1,0,2:T(2,128)(2,1)S(1)} %broadcast_select_fusion.15), channel_id=1, source_target_pairs={{2,0},{4,2},{6,4},{3,1},{5,3},{7,5},{10,8},{12,10},{14,12},{11,9},... | collective-permute-start | bytes 393224 | tf_op jit(solution)/shard_map/ppermute | solution.py:19
  144.1 7.1 %collective-permute-start.9 = (bf16[256,2,1,128]{3,1,0,2:T(2,128)(2,1)S(1)}, bf16[256,2,1,128]{3,1,0,2:T(2,128)(2,1)S(1)}, u32[]{:S(2)}, u32[]{:S(2)}) collective-permute-start(bf16[256,2,1,128]{3,1,0,2:T(2,128)(2,1)S(1)} %broadcast_select_fusion.15), channel_id=1, source_target_pairs={{0,2},{2,4},{4,6},{1,3},{3,5},{5,7},{8,10},{10,12},{12,14},{9,11},... | collective-permute-start | bytes 393224 | tf_op jit(solution)/shard_map/ppermute | solution.py:17
  151.2 4.4 copy-start.10
  171.2 55.4 %reduce-scatter.16.cloned.1.call-start = ((), (), s32[]{:S(2)}) async-start(), calls=%async_computation.11 | async-start | bytes 393216 | tf_op jit(solution)/shard_map/reduce_scatter | solution.py:93
  183.7 6.9 %collective-permute-start.11 = (bf16[256,2,1,128]{3,1,0,2:T(2,128)(2,1)S(1)}, bf16[256,2,1,128]{3,1,0,2:T(2,128)(2,1)S(1)}, u32[]{:S(2)}, u32[]{:S(2)}) collective-permute-start(bf16[256,2,1,128]{3,1,0,2:T(2,128)(2,1)S(1)} %get-tuple-element.278), channel_id=1, source_target_pairs={{0,8},{8,16},{16,24},{1,9},{9,17},{17,25},{2,10},{10,18},{18,26},{... | collective-permute-start | bytes 393224 | tf_op jit(solution)/shard_map/ppermute | solution.py:29
  190.8 5.9 collective-permute-start.12
  194.2 6.9 %collective-permute-start.13 = (bf16[256,2,1,128]{3,1,0,2:T(2,128)(2,1)S(1)}, bf16[256,2,1,128]{3,1,0,2:T(2,128)(2,1)S(1)}, u32[]{:S(2)}, u32[]{:S(2)}) collective-permute-start(bf16[256,2,1,128]{3,1,0,2:T(2,128)(2,1)S(1)} %broadcast_select_fusion.14), channel_id=1, source_target_pairs={{2,0},{4,2},{6,4},{3,1},{5,3},{7,5},{10,8},{12,10},{14,12},{11,9},... | collective-permute-start | bytes 393224 | tf_op jit(solution)/shard_map/ppermute | solution.py:19
  211.7 63.8 %reduce-scatter.18.cloned.1.call-start = ((), (), s32[]{:S(2)}) async-start(), calls=%async_computation.12 | async-start | bytes 393216 | tf_op jit(solution)/shard_map/reduce_scatter | solution.py:93
  228.4 6.8 %collective-permute-start.14 = (bf16[256,2,1,128]{3,1,0,2:T(2,128)(2,1)S(1)}, bf16[256,2,1,128]{3,1,0,2:T(2,128)(2,1)S(1)}, u32[]{:S(2)}, u32[]{:S(2)}) collective-permute-start(bf16[256,2,1,128]{3,1,0,2:T(2,128)(2,1)S(1)} %get-tuple-element.274), channel_id=1, source_target_pairs={{0,8},{8,16},{16,24},{1,9},{9,17},{17,25},{2,10},{10,18},{18,26},{... | collective-permute-start | bytes 393224 | tf_op jit(solution)/shard_map/ppermute | solution.py:29
  235.5 5.9 collective-permute-start.15
  238.9 7.0 %collective-permute-start.16 = (bf16[256,2,1,128]{3,1,0,2:T(2,128)(2,1)S(1)}, bf16[256,2,1,128]{3,1,0,2:T(2,128)(2,1)}, u32[]{:S(2)}, u32[]{:S(2)}) collective-permute-start(bf16[256,2,1,128]{3,1,0,2:T(2,128)(2,1)S(1)} %broadcast_select_fusion.13), channel_id=1, source_target_pairs={{2,0},{4,2},{6,4},{3,1},{5,3},{7,5},{10,8},{12,10},{14,12},{11,9},... | collective-permute-start | bytes 393224 | tf_op jit(solution)/shard_map/ppermute | solution.py:19
  260.6 127.9 %reduce-scatter.20.cloned.1.call-start = ((), (), s32[]{:S(2)}) async-start(), calls=%async_computation.13 | async-start | bytes 393216 | tf_op jit(solution)/shard_map/reduce_scatter | solution.py:93
  277.3 6.8 %collective-permute-start.17 = (bf16[256,2,1,128]{3,1,0,2:T(2,128)(2,1)S(1)}, bf16[256,2,1,128]{3,1,0,2:T(2,128)(2,1)S(1)}, u32[]{:S(2)}, u32[]{:S(2)}) collective-permute-start(bf16[256,2,1,128]{3,1,0,2:T(2,128)(2,1)S(1)} %get-tuple-element.272), channel_id=1, source_target_pairs={{0,8},{8,16},{16,24},{1,9},{9,17},{17,25},{2,10},{10,18},{18,26},{... | collective-permute-start | bytes 393224 | tf_op jit(solution)/shard_map/ppermute | solution.py:29
  284.3 5.9 collective-permute-start.18
  287.7 6.9 %collective-permute-start.19 = (bf16[256,2,1,128]{3,1,0,2:T(2,128)(2,1)S(1)}, bf16[256,2,1,128]{3,1,0,2:T(2,128)(2,1)S(1)}, u32[]{:S(2)}, u32[]{:S(2)}) collective-permute-start(bf16[256,2,1,128]{3,1,0,2:T(2,128)(2,1)S(1)} %broadcast_select_fusion.12), channel_id=1, source_target_pairs={{2,0},{4,2},{6,4},{3,1},{5,3},{7,5},{10,8},{12,10},{14,12},{11,9},... | collective-permute-start | bytes 393224 | tf_op jit(solution)/shard_map/ppermute | solution.py:19
  305.1 351.7 %all-reduce.10.cloned.1.call-start = ((), (), s32[]{:S(2)}) async-start(), calls=%async_computation.14 | async-start | bytes 14155776 | tf_op jit(solution)/shard_map/psum | solution.py:122
  390.3 273.3 %copy-start.19 = (bf16[1,256,8,1,128]{4,2,3,1,0:T(8,128)(2,1)}, bf16[1,256,8,1,128]{4,2,3,1,0:T(8,128)(2,1)S(1)}, u32[]{:S(2)}) copy-start(bf16[1,256,8,1,128]{4,2,3,1,0:T(8,128)(2,1)S(1)} %fusion.88) | copy-start | bytes 1572868
  (13 other events, 21.3 us)
Sparse Core Ops, SparseCore 0:
  37.5 6.0 reduce-scatter.7
  81.7 7.7 reduce-scatter.9
  125.3 8.6 reduce-scatter.11
  171.3 10.5 reduce-scatter.13
  211.8 14.7 reduce-scatter.15
  260.8 14.6 reduce-scatter.17
  305.3 14.6 reduce-scatter.19
  388.6 268.2 all-reduce.9
where the time goes:
time: 680 us; the launch traced here: 671 us
  waiting for transfers between devices  383 us (56%)
  local copies, waits for them, and re-layouts  102 us (15%)
  matrix products  68.4 us (10%)
  starting transfers between devices  59.2 us (9%)
  other arithmetic  35.4 us (5%)
  between operations  15.4 us (2%)
  loops' own time  7.48 us (1%)
    psum x1, waiting for transfers between devices, body(): kernel_total = lax.psum(kernel_sum.astype(jnp.bfloat16), 'frame')  267 us
    unnamed x216, local copies, waits for them, and re-layouts  73.7 us
    reduce_scatter x7, waiting for transfers between devices, body(): lax.psum_scatter(lax.cond(active, busy, resting, 0).astype(jnp.bfloat16),...  63.1 us
    dot_general x4, matrix products, add_kernel(): lax.dot_general(taps_mat, features, (((1,), (1,)), ((), ())), preferred_e...  44 us
    ppermute x7, waiting for transfers between devices, with_halo(): lax.ppermute(head, axis, [((i + 1) % count, i) for i in range(ends)])  26.8 us
    ppermute x7, starting transfers between devices, with_halo(): lax.ppermute(tail, axis, [(i, (i + 1) % count) for i in range(ends)])  26.7 us
    dot_general x4, matrix products, busy(): lax.dot_general(kernel_mat, taps_mat, (((0,), (0,)), ((), ())), preferred...  24.4 us
    ppermute x6, starting transfers between devices, shifted(): lax.ppermute(value, axis, [(source, source + steps) for source in range(l...  21.7 us
  transfers between devices with their start and end apart: 28, of which 27 were waited for; matrix products, arithmetic and copies ran while one was open for 12% of the time, Pallas kernels for 0%

commit v1 on v0

v1 whole, which is shorter than its diff:
```python
import jax
import jax.numpy as jnp
from jax import lax
from jax.experimental import pallas as pl
from jax.experimental.pallas import tpu as pltpu
from jax.sharding import PartitionSpec as P

BLOCK_FRAMES = 2
F32 = jnp.float32
BF16 = jnp.bfloat16


def back_kernel(cur_ref, later_ref, w_ref, out_ref, spread, acc):
    step = pl.program_id(0)
    frames_n, rows_n, width_n, group = cur_ref.shape

    @pl.when(step == 0)
    def _():
        acc[...] = jnp.zeros_like(acc)
        empty = jnp.zeros((width_n, 3 * group), F32)
        for frame in range(2 * frames_n):
            spread[frame, 0] = empty
            spread[frame, rows_n + 1] = empty
            for row in range(rows_n):
                source = cur_ref[frame, row] if frame < frames_n else later_ref[frame - frames_n, row]
                cells = source.astype(F32)
                spread[frame, row + 1, :, 0:group] = pltpu.roll(cells, width_n - 1, 0)
                spread[frame, row + 1, :, group : 2 * group] = cells
                spread[frame, row + 1, :, 2 * group : 3 * group] = pltpu.roll(cells, 1, 0)

    lag = step // 3
    offset = 2 - step % 3
    taken = spread[pl.ds(lag, frames_n), pl.ds(offset, rows_n)]
    taken = taken.reshape(frames_n * rows_n * width_n, 3 * group).astype(BF16)
    acc[...] += jnp.dot(taken, w_ref[...].reshape(3 * group, -1), preferred_element_type=F32)

    @pl.when(step == pl.num_programs(0) - 1)
    def _():
        out_ref[...] = acc[...].astype(BF16)


def back_block(current, later, kernels):
    frames_n, rows_n, width_n, group = current.shape
    channels = kernels.shape[2]
    cells = frames_n * rows_n * width_n
    whole = pl.BlockSpec(current.shape, lambda step: (0, 0, 0, 0))
    return pl.pallas_call(
        back_kernel,
        grid=(9,),
        in_specs=[whole, whole, pl.BlockSpec((3, group, channels), lambda step: (step, 0, 0))],
        out_specs=pl.BlockSpec((cells, channels), lambda step: (0, 0)),
        out_shape=jax.ShapeDtypeStruct((cells, channels), BF16),
        scratch_shapes=[
            pltpu.VMEM((2 * frames_n, rows_n + 2, width_n, 3 * group), F32),
            pltpu.VMEM((cells, channels), F32),
        ],
        compiler_params=pltpu.CompilerParams(vmem_limit_bytes=30 * 2**20),
        cost_estimate=pl.CostEstimate(
            flops=54 * group * channels * cells, bytes_accessed=54 * group * channels, transcendentals=0
        ),
    )(current, later, kernels)


def tap_kernel(grad_ref, parts_ref, out_ref, feature_ref, arrived):
    tap = pl.program_id(0)
    rings, chans, rows_l, _, width_c = parts_ref.shape

    @pl.when(tap == 0)
    def _():
        copies = []
        for ring in range(rings):
            for chan in range(chans):
                copies.append(
                    pltpu.make_async_copy(
                        parts_ref.at[ring, chan],
                        feature_ref.at[pl.ds(ring * rows_l, rows_l), :, pl.ds(chan * width_c, width_c)],
                        arrived.at[ring * chans + chan],
                    )
                )
        for copy in copies:
            copy.start()
        for copy in copies:
            copy.wait()

    lag = tap // 9
    offset = 2 - (tap // 3) % 3
    side = tap % 3
    rows_n, span = feature_ref.shape[0], feature_ref.shape[1]
    padded = span + 2 * 128
    total = jnp.zeros(out_ref.shape[1:], F32)
    for row in range(rows_n):
        start = pl.multiple_of((row + offset) * padded + lag * 128, 128)
        total += jnp.dot(grad_ref[side, :, pl.ds(start, span)], feature_ref[row], preferred_element_type=F32)
    out_ref[0] = total.astype(BF16)


def kernel_gradient(grads, parts):
    group = grads.shape[1]
    rings, chans, rows_l, span, width_c = parts.shape
    channels = chans * width_c
    return pl.pallas_call(
        tap_kernel,
        grid=(27,),
        in_specs=[
            pl.BlockSpec(grads.shape, lambda tap: (0, 0, 0), pipeline_mode=pl.Buffered(1)),
            pl.BlockSpec(memory_space=pl.ANY),
        ],
        out_specs=pl.BlockSpec((1, group, channels), lambda tap: (tap, 0, 0)),
        out_shape=jax.ShapeDtypeStruct((27, group, channels), BF16),
        scratch_shapes=[
            pltpu.VMEM((rings * rows_l, span, channels), BF16),
            pltpu.SemaphoreType.DMA((rings * chans,)),
        ],
        compiler_params=pltpu.CompilerParams(vmem_limit_bytes=48 * 2**20),
        cost_estimate=pl.CostEstimate(
            flops=54 * group * parts.size,
            bytes_accessed=2 * (grads.size + parts.size + 27 * group * channels),
            transcendentals=0,
        ),
    )(grads, parts)


def body(upstream, acts, weights):
    group, frames_all, rows_l, width_n = upstream.shape
    channels = acts.shape[1]
    sections, rings, chans = lax.axis_size("section"), lax.axis_size("frame"), lax.axis_size("chan")
    section_pos, ring_pos, chan_pos = lax.axis_index("section"), lax.axis_index("frame"), lax.axis_index("chan")
    rows_n = rows_l * rings
    own = width_n // rings
    halo = sections
    window = own + 2 * halo
    blocks_n = frames_all // BLOCK_FRAMES
    ticks = blocks_n + sections - 1
    kernels = weights[0]

    mine = lax.dynamic_slice_in_dim(acts[0], chan_pos * group, group, 0)
    shared = group % 128 == 0
    values = (mine if shared else acts[0]).astype(F32)
    feature_part = (values * jax.nn.sigmoid(values)).astype(BF16).transpose(2, 1, 3, 0)
    feature_part = feature_part.reshape(rows_l, frames_all * width_n, -1)
    feature_all = lax.all_gather(feature_part, ("frame", "chan") if shared else "frame")
    feature_all = feature_all.reshape(rings, chans if shared else 1, *feature_part.shape)

    both = jnp.stack([upstream, mine]).transpose(2, 0, 3, 4, 1)
    both = jnp.pad(both, ((0, 0), (0, 0), (0, 0), (halo, halo), (0, 0)))
    windows = jnp.stack([both[:, :, :, own * i : own * i + window] for i in range(rings)])
    fresh, stored = [], []
    for order in range(blocks_n):
        first = (blocks_n - 1 - order) * BLOCK_FRAMES
        piece = lax.all_to_all(windows[:, first : first + BLOCK_FRAMES], "frame", 0, 0)
        piece = piece.transpose(2, 1, 0, 3, 4, 5).reshape(2, BLOCK_FRAMES, rows_n, window, group)
        fresh.append(piece[0])
        stored.append(piece[1])

    column = ring_pos * own - halo + jnp.arange(window)
    inside = jnp.logical_and(column >= 0, column < width_n)[None, None, :, None]
    later = jnp.zeros((BLOCK_FRAMES, rows_n, window, group), BF16)
    inbound = later
    gathered, results = [], []
    for tick in range(ticks):
        if tick < blocks_n:
            current = jnp.where(section_pos == 0, fresh[tick], inbound)
        else:
            current = inbound
        gathered.append(lax.all_gather(current[:, :, halo : halo + own], "frame"))
        partial = back_block(current, later, kernels)
        summed = lax.dynamic_slice_in_dim(partial, chan_pos * group, group, 1).astype(F32)
        for step in range(1, chans):
            there = lax.rem(chan_pos + step, chans)
            piece = lax.dynamic_slice_in_dim(partial, there * group, group, 1)
            arrived = lax.ppermute(piece, "chan", [(i, (i + step) % chans) for i in range(chans)])
            summed = summed + arrived.astype(F32)
        known = jnp.stack(stored[: tick + 1])
        place = jnp.clip(tick - section_pos, 0, known.shape[0] - 1)
        slot = lax.dynamic_index_in_dim(known, place, 0, keepdims=False).astype(F32)
        logistic = jax.nn.sigmoid(slot)
        slope = logistic * (1.0 + slot * (1.0 - logistic))
        updated = current.astype(F32) + slope * summed.reshape(current.shape)
        updated = jnp.where(inside, updated, 0.0).astype(BF16)
        results.append(updated[:, :, halo : halo + own])
        later = current
        if tick + 1 < ticks:
            inbound = lax.ppermute(updated, "section", [(i, i + 1) for i in range(sections - 1)])

    taken = lax.dynamic_slice_in_dim(jnp.stack(gathered), section_pos, blocks_n, 0)[::-1]
    whole = taken.transpose(5, 3, 0, 2, 1, 4).reshape(group, rows_n, frames_all, width_n)
    padded = jnp.pad(whole, ((0, 0), (1, 1), (0, 2), (1, 1)))
    sides = jnp.stack([padded[..., 2 - j : 2 - j + width_n] for j in range(3)])
    sides = sides.reshape(3, group, -1)
    kernel_total = kernel_gradient(sides, feature_all)

    outs = lax.dynamic_slice_in_dim(jnp.stack(results), section_pos, blocks_n, 0)[::-1]
    outs = outs.reshape(frames_all, rings, rows_l, own, group).transpose(1, 0, 2, 3, 4)
    outs = lax.all_to_all(outs, "frame", 0, 0)
    outs = outs.transpose(4, 1, 2, 0, 3).reshape(group, frames_all, rows_l, width_n)
    return (outs[None], kernel_total[None])


def solution(mesh):
    placed = (
        P("chan", None, "frame", None),
        P("section", None, None, "frame", None),
        P("section", None, "chan", None),
    )
    return jax.shard_map(
        body,
        mesh=mesh,
        in_specs=placed,
        out_specs=(P("section", "chan", None, "frame", None), P("section", None, "chan", None)),
        check_vma=False,
    )
```

time: 680 us -> 373 us (0.55)
  waiting for transfers between devices: 383 us -> 57.5 us
  blocking collectives: 0 us -> 132 us
  Pallas kernels: 0 us -> 68.5 us
  matrix products: 68.4 us -> 0 us
  local copies, waits for them, and re-layouts: 102 us -> 41.1 us
  other arithmetic: 35.4 us -> 13.4 us
  starting transfers between devices: 59.2 us -> 42.4 us
  loops' own time: 7.48 us -> 0 us
    psum x1 -> x0, waiting for transfers between devices: 267 us -> none  [body(): kernel_total = lax.psum(kernel_sum.astype(jnp.bfloat16), 'frame')]
    all_gather x0 -> x7, blocking collectives: none -> 116 us  [body(): gathered.append(lax.all_gather(current[:, :, halo:halo + own], 'frame'))]
    pallas_call x0 -> x8, Pallas kernels: none -> 68.5 us  [the longest x1 39.6 us: kernel_gradient(): pl.pallas_call(tap_kernel, grid=(27,), in_specs=[pl.BlockSpec(grads.shape...]
    dot_general x8 -> x0, matrix products: 68.4 us -> none  [the longest x4 44 us: add_kernel(): lax.dot_general(taps_mat, features, (((1,), (1,)), ((), ())), preferred_e...]
    reduce_scatter x7 -> x0, waiting for transfers between devices: 63.1 us -> none  [body(): lax.psum_scatter(lax.cond(active, busy, resting, 0).astype(jnp.bfloat16),...]
    unnamed x216 -> x25, local copies, waits for them, and re-layouts: 73.7 us -> 12.6 us
    all_to_all x0 -> x4, waiting for transfers between devices: none -> 40.8 us  [the longest x3 38 us: body(): lax.all_to_all(windows[:, first:first + BLOCK_FRAMES], 'frame', 0, 0)]
    ppermute x20 -> x13, waiting for transfers between devices: 52.8 us -> 16.6 us  [the longest x6 16.6 us: body(): lax.ppermute(updated, 'section', [(i, i + 1) for i in range(sections - 1)])]
  transfers between devices with their start and end apart: 28 -> 18, of which waited for: 27 -> 10; matrix products, arithmetic and copies ran while one was open for 12% -> 11% of each run, Pallas kernels for 0% -> 8%
where the time goes in v1:
time: 373 us; the launch traced here: 370 us
  blocking collectives  132 us (35%)
  Pallas kernels  68.5 us (18%)
  waiting for transfers between devices  57.5 us (15%)
  starting transfers between devices  42.4 us (11%)
  local copies, waits for them, and re-layouts  41.1 us (11%)
  between operations  14.8 us (4%)
  other arithmetic  13.4 us (4%)
    all_gather x7, blocking collectives, body(): gathered.append(lax.all_gather(current[:, :, halo:halo + own], 'frame'))  116 us
    pallas_call x1, Pallas kernels, kernel_gradient(): pl.pallas_call(tap_kernel, grid=(27,), in_specs=[pl.BlockSpec(grads.shape...  39.6 us
    all_to_all x3, waiting for transfers between devices, body(): lax.all_to_all(windows[:, first:first + BLOCK_FRAMES], 'frame', 0, 0)  38 us
    pallas_call x7, Pallas kernels, back_block(): pl.pallas_call(back_kernel, grid=(9,), in_specs=[whole, whole, pl.BlockSp...  28.9 us
    ppermute x6, starting transfers between devices, body(): lax.ppermute(updated, 'section', [(i, i + 1) for i in range(sections - 1)])  28 us
    another operation x3, local copies, waits for them, and re-layouts, body(): sides = jnp.stack([padded[..., 2 - j:2 - j + width_n] for j in range(3)])  18.7 us
    ppermute x6, waiting for transfers between devices, body(): lax.ppermute(updated, 'section', [(i, i + 1) for i in range(sections - 1)])  16.6 us
    all_to_all x1, blocking collectives, body(): lax.all_to_all(windows[:, first:first + BLOCK_FRAMES], 'frame', 0, 0)  16.4 us
  transfers between devices with their start and end apart: 18, of which 10 were waited for; matrix products, arithmetic and copies ran while one was open for 11% of the time, Pallas kernels for 8%

profile of v1, /device:TPU:0, one launch (start us, length us, event | category | flops | bytes accessed | tf_op | source)
XLA Modules:
  0.0 369.8 jit_solution(14273320723875966444)
XLA Ops:
  12.1 16.4 %all_to_all.25 = bf16[4,2,2,1,40,256]{5,4,1,3,2,0:T(8,128)(2,1)S(1)} all-to-all(bf16[4,2,2,1,40,256]{5,4,1,3,2,0:T(8,128)(2,1)S(1)} %get-tuple-element.14), channel_id=1, replica_groups=mesh['section'=4,'frame'=4,'chan'=2] {'frame'}, dimensions={0} | all-to-all | bytes 655360 | tf_op jit(solution)/shard_map/all_to_all | solution.py:150
  33.1 7.8 %all-to-all-done.1 = bf16[4,2,2,1,40,256]{5,4,1,3,2,0:T(8,128)(2,1)S(1)} async-done(((bf16[4,2,2,1,40,256]{5,4,1,3,2,0:T(8,128)(2,1)}), bf16[4,2,2,1,40,256]{5,4,1,3,2,0:T(8,128)(2,1)S(1)}, u32[]{:S(2)}, u32[]{:S(2)}) %all-to-all-start.1) | async-done | bytes 327712 | tf_op jit(solution)/shard_map/all_to_all | solution.py:150
  40.9 3.5 all-to-all-start.2
  47.6 4.1 %shard_map.50 = bf16[320,512]{1,0:T(8,128)(2,1)S(1)} custom-call(bf16[2,4,40,256]{3,2,1,0:T(8,128)(2,1)S(1)} %get-tuple-element.23.cur_ref.later_ref, bf16[2,4,40,256]{3,2,1,0:T(8,128)(2,1)S(1)} %broadcast_in_dim.47.later_ref, bf16[27,256,512]{2,1,0:T(8,128)(2,1)S(1)} %bitcast.144), custom_call_target="tpu_custom_call" | custom-call | flops 2264924160 | bytes 7077888 | tf_op jit(solution)/shard_map/pallas_call | solution.py:47
  51.7 10.7 %all-to-all-done.2 = bf16[4,2,2,1,40,256]{5,4,1,3,2,0:T(8,128)(2,1)S(1)} async-done(((bf16[4,2,2,1,40,256]{5,4,1,3,2,0:T(8,128)(2,1)}), bf16[4,2,2,1,40,256]{5,4,1,3,2,0:T(8,128)(2,1)S(1)}, u32[]{:S(2)}, u32[]{:S(2)}) %all-to-all-start.2) | async-done | bytes 327712 | tf_op jit(solution)/shard_map/all_to_all | solution.py:150
  62.4 3.5 all-to-all-start.3
  66.1 19.5 %all-to-all-done.3 = bf16[4,2,2,1,40,256]{5,4,1,3,2,0:T(8,128)(2,1)S(1)} async-done(((bf16[4,2,2,1,40,256]{5,4,1,3,2,0:T(8,128)(2,1)}), bf16[4,2,2,1,40,256]{5,4,1,3,2,0:T(8,128)(2,1)S(1)}, u32[]{:S(2)}, u32[]{:S(2)}) %all-to-all-start.3) | async-done | bytes 327712 | tf_op jit(solution)/shard_map/all_to_all | solution.py:150
  85.6 18.6 %all-gather = bf16[8,4,32,256]{3,2,1,0:T(8,128)(2,1)S(1)} all-gather(bf16[2,4,32,256]{3,2,1,0:T(8,128)(2,1)S(1)} %slice.179), channel_id=2, replica_groups=mesh['section'=4,'frame'=4,'chan'=2] {'frame'}, dimensions={0}, use_global_device_ids=true | all-gather | bytes 655360 | tf_op jit(solution)/shard_map/all_gather | solution.py:165
  113.9 4.1 %shard_map.51 = bf16[320,512]{1,0:T(8,128)(2,1)S(1)} custom-call(bf16[2,4,40,256]{3,2,1,0:T(8,128)(2,1)S(1)} %fusion.73.cur_ref.later_ref, bf16[2,4,40,256]{3,2,1,0:T(8,128)(2,1)S(1)} %get-tuple-element.23.cur_ref.later_ref, bf16[27,256,512]{2,1,0:T(8,128)(2,1)S(1)} %bitcast.145), custom_call_target="tpu_custom_call" | custom-call | flops 2264924160 | bytes 7077888 | tf_op jit(solution)/shard_map/pallas_call | solution.py:47
  118.1 16.2 %all-gather.1 = bf16[8,4,32,256]{3,2,1,0:T(8,128)(2,1)S(1)} all-gather(bf16[2,4,32,256]{3,2,1,0:T(8,128)(2,1)S(1)} %slice.180), channel_id=3, replica_groups=mesh['section'=4,'frame'=4,'chan'=2] {'frame'}, dimensions={0}, use_global_device_ids=true | all-gather | bytes 655360 | tf_op jit(solution)/shard_map/all_gather | solution.py:165
  134.7 4.4 %collective-permute-start.3 = (bf16[2,4,40,256]{3,2,1,0:T(8,128)(2,1)S(1)}, bf16[2,4,40,256]{3,2,1,0:T(8,128)(2,1)S(1)}, u32[]{:S(2)}, u32[]{:S(2)}) collective-permute-start(bf16[2,4,40,256]{3,2,1,0:T(8,128)(2,1)S(1)} %fusion.21), channel_id=1, source_target_pairs={{0,8},{8,16},{16,24},{1,9},{9,17},{17,25},{2,10},{10,18},{18,26},{... | collective-permute-start | bytes 491528 | tf_op jit(solution)/shard_map/ppermute | solution.py:183
  141.9 4.1 %shard_map.52 = bf16[320,512]{1,0:T(8,128)(2,1)S(1)} custom-call(bf16[2,4,40,256]{3,2,1,0:T(8,128)(2,1)S(1)} %fusion.72.cur_ref.later_ref, bf16[2,4,40,256]{3,2,1,0:T(8,128)(2,1)S(1)} %fusion.73.cur_ref.later_ref, bf16[27,256,512]{2,1,0:T(8,128)(2,1)S(1)} %bitcast.146), custom_call_target="tpu_custom_call" | custom-call | flops 2264924160 | bytes 7077888 | tf_op jit(solution)/shard_map/pallas_call | solution.py:47
  146.2 16.2 %all-gather.2 = bf16[8,4,32,256]{3,2,1,0:T(8,128)(2,1)S(1)} all-gather(bf16[2,4,32,256]{3,2,1,0:T(8,128)(2,1)S(1)} %slice.181), channel_id=4, replica_groups=mesh['section'=4,'frame'=4,'chan'=2] {'frame'}, dimensions={0}, use_global_device_ids=true | all-gather | bytes 655360 | tf_op jit(solution)/shard_map/all_gather | solution.py:165
  162.8 4.4 %collective-permute-start.5 = (bf16[2,4,40,256]{3,2,1,0:T(8,128)(2,1)S(1)}, bf16[2,4,40,256]{3,2,1,0:T(8,128)(2,1)S(1)}, u32[]{:S(2)}, u32[]{:S(2)}) collective-permute-start(bf16[2,4,40,256]{3,2,1,0:T(8,128)(2,1)S(1)} %fusion.30), channel_id=1, source_target_pairs={{0,8},{8,16},{16,24},{1,9},{9,17},{17,25},{2,10},{10,18},{18,26},{... | collective-permute-start | bytes 491528 | tf_op jit(solution)/shard_map/ppermute | solution.py:183
  170.0 4.1 %shard_map.53 = bf16[320,512]{1,0:T(8,128)(2,1)S(1)} custom-call(bf16[2,4,40,256]{3,2,1,0:T(8,128)(2,1)S(1)} %fusion.71.cur_ref.later_ref, bf16[2,4,40,256]{3,2,1,0:T(8,128)(2,1)S(1)} %fusion.72.cur_ref.later_ref, bf16[27,256,512]{2,1,0:T(8,128)(2,1)S(1)} %bitcast.147), custom_call_target="tpu_custom_call" | custom-call | flops 2264924160 | bytes 7077888 | tf_op jit(solution)/shard_map/pallas_call | solution.py:47
  174.3 16.2 %all-gather.3 = bf16[8,4,32,256]{3,2,1,0:T(8,128)(2,1)S(1)} all-gather(bf16[2,4,32,256]{3,2,1,0:T(8,128)(2,1)S(1)} %slice.182), channel_id=5, replica_groups=mesh['section'=4,'frame'=4,'chan'=2] {'frame'}, dimensions={0}, use_global_device_ids=true | all-gather | bytes 655360 | tf_op jit(solution)/shard_map/all_gather | solution.py:165
  190.8 5.2 %collective-permute-start.7 = (bf16[2,4,40,256]{3,2,1,0:T(8,128)(2,1)S(1)}, bf16[2,4,40,256]{3,2,1,0:T(8,128)(2,1)S(1)}, u32[]{:S(2)}, u32[]{:S(2)}) collective-permute-start(bf16[2,4,40,256]{3,2,1,0:T(8,128)(2,1)S(1)} %fusion.39), channel_id=1, source_target_pairs={{0,8},{8,16},{16,24},{1,9},{9,17},{17,25},{2,10},{10,18},{18,26},{... | collective-permute-start | bytes 491528 | tf_op jit(solution)/shard_map/ppermute | solution.py:183
  198.8 4.1 %shard_map.54 = bf16[320,512]{1,0:T(8,128)(2,1)S(1)} custom-call(bf16[2,4,40,256]{3,2,1,0:T(8,128)(2,1)S(1)} %collective-permute-done.7.cur_ref.later_ref, bf16[2,4,40,256]{3,2,1,0:T(8,128)(2,1)S(1)} %fusion.71.cur_ref.later_ref, bf16[27,256,512]{2,1,0:T(8,128)(2,1)S(1)} %bitcast.148), custom_call_target="tpu_custom_call" | custom-call | flops 2264924160 | bytes 7077888 | tf_op jit(solution)/shard_map/pallas_call | solution.py:47
  203.1 16.2 %all-gather.4 = bf16[8,4,32,256]{3,2,1,0:T(8,128)(2,1)S(1)} all-gather(bf16[2,4,32,256]{3,2,1,0:T(8,128)(2,1)S(1)} %slice.183), channel_id=6, replica_groups=mesh['section'=4,'frame'=4,'chan'=2] {'frame'}, dimensions={0}, use_global_device_ids=true | all-gather | bytes 655360 | tf_op jit(solution)/shard_map/all_gather | solution.py:165
  219.6 5.3 %collective-permute-start.9 = (bf16[2,4,40,256]{3,2,1,0:T(8,128)(2,1)S(1)}, bf16[2,4,40,256]{3,2,1,0:T(8,128)(2,1)S(1)}, u32[]{:S(2)}, u32[]{:S(2)}) collective-permute-start(bf16[2,4,40,256]{3,2,1,0:T(8,128)(2,1)S(1)} %fusion.48), channel_id=1, source_target_pairs={{0,8},{8,16},{16,24},{1,9},{9,17},{17,25},{2,10},{10,18},{18,26},{... | collective-permute-start | bytes 491528 | tf_op jit(solution)/shard_map/ppermute | solution.py:183
  227.7 4.1 %shard_map.55 = bf16[320,512]{1,0:T(8,128)(2,1)S(1)} custom-call(bf16[2,4,40,256]{3,2,1,0:T(8,128)(2,1)S(1)} %collective-permute-done.9.cur_ref.later_ref, bf16[2,4,40,256]{3,2,1,0:T(8,128)(2,1)S(1)} %collective-permute-done.7.cur_ref.later_ref, bf16[27,256,512]{2,1,0:T(8,128)(2,1)S(1)} %bitcast.149), custom_call_target="tpu_custom_call" | custom-call | flops 2264924160 | bytes 7077888 | tf_op jit(solution)/shard_map/pallas_call | solution.py:47
  231.9 16.2 %all-gather.5 = bf16[8,4,32,256]{3,2,1,0:T(8,128)(2,1)S(1)} all-gather(bf16[2,4,32,256]{3,2,1,0:T(8,128)(2,1)S(1)} %slice.184), channel_id=7, replica_groups=mesh['section'=4,'frame'=4,'chan'=2] {'frame'}, dimensions={0}, use_global_device_ids=true | all-gather | bytes 655360 | tf_op jit(solution)/shard_map/all_gather | solution.py:165
  248.5 5.3 %collective-permute-start.11 = (bf16[2,4,40,256]{3,2,1,0:T(8,128)(2,1)S(1)}, bf16[2,4,40,256]{3,2,1,0:T(8,128)(2,1)S(1)}, u32[]{:S(2)}, u32[]{:S(2)}) collective-permute-start(bf16[2,4,40,256]{3,2,1,0:T(8,128)(2,1)S(1)} %get-tuple-element.21), channel_id=1, source_target_pairs={{0,8},{8,16},{16,24},{1,9},{9,17},{17,25},{2,10},{10,18},{18,26},{... | collective-permute-start | bytes 491528 | tf_op jit(solution)/shard_map/ppermute | solution.py:183
  256.6 4.1 %shard_map.56 = bf16[320,512]{1,0:T(8,128)(2,1)S(1)} custom-call(bf16[2,4,40,256]{3,2,1,0:T(8,128)(2,1)S(1)} %collective-permute-done.11.cur_ref, bf16[2,4,40,256]{3,2,1,0:T(8,128)(2,1)S(1)} %collective-permute-done.9.cur_ref.later_ref, bf16[27,256,512]{2,1,0:T(8,128)(2,1)S(1)} %bitcast.150), custom_call_target="tpu_custom_call" | custom-call | flops 2264924160 | bytes 7077888 | tf_op jit(solution)/shard_map/pallas_call | solution.py:47
  260.9 16.4 %all-gather.6 = bf16[8,4,32,256]{3,2,1,0:T(8,128)(2,1)S(1)} all-gather(bf16[2,4,32,256]{3,2,1,0:T(8,128)(2,1)S(1)} %slice.176), channel_id=8, replica_groups=mesh['section'=4,'frame'=4,'chan'=2] {'frame'}, dimensions={0}, use_global_device_ids=true | all-gather | bytes 655360 | tf_op jit(solution)/shard_map/all_gather | solution.py:165
  278.0 5.8 %pad_slice_fusion.2 = (bf16[256,6,10,128]{0,3,2,1:T(8,128)(2,1)}, bf16[256,6,10,128]{0,3,2,1:T(8,128)(2,1)}, bf16[256,6,10,128]{0,3,2,1:T(8,128)(2,1)}) fusion(bf16[256,4,8,128]{0,3,2,1:T(8,128)(2,1)S(1)} %bitcast.155), kind=kLoop, calls=%fused_computation.3 | loop fusion | bytes 13893632 | tf_op jit(solution)/shard_map/slice | solution.py:188
  283.8 6.2 %copy.59 = bf16[1,256,7680]{2,1,0:T(8,128)(2,1)} copy(bf16[1,256,7680]{1,2,0:T(8,128)(2,1)} %bitcast.154) | data formatting | bytes 7864320 | tf_op jit(solution)/shard_map/stack | solution.py:188
  290.0 6.2 %copy.58 = bf16[1,256,7680]{2,1,0:T(8,128)(2,1)} copy(bf16[1,256,7680]{1,2,0:T(8,128)(2,1)} %bitcast.153) | data formatting | bytes 7864320 | tf_op jit(solution)/shard_map/stack | solution.py:188
  296.2 6.3 %copy.57 = bf16[1,256,7680]{2,1,0:T(8,128)(2,1)} copy(bf16[1,256,7680]{1,2,0:T(8,128)(2,1)} %bitcast.152) | data formatting | bytes 7864320 | tf_op jit(solution)/shard_map/stack | solution.py:188
  303.7 3.5 all-to-all-start.4
  307.1 10.1 %pad_maximum_fusion.grad_ref = bf16[3,256,7680]{2,1,0:T(8,128)(2,1)} fusion(bf16[1,256,7680]{2,1,0:T(8,128)(2,1)} %copy.59, bf16[1,256,7680]{2,1,0:T(8,128)(2,1)} %copy.58, bf16[1,256,7680]{2,1,0:T(8,128)(2,1)} %copy.57), kind=kLoop, calls=%fused_computation | loop fusion | flops 11796480 | bytes 23592960 | tf_op jit(solution)/shard_map/stack | solution.py:188
  323.4 39.6 %shard_map.57 = bf16[27,256,512]{2,1,0:T(8,128)(2,1)} custom-call(bf16[3,256,7680]{2,1,0:T(8,128)(2,1)} %pad_maximum_fusion.grad_ref, bf16[4,2,1,1024,256]{4,3,2,1,0:T(8,128)(2,1)S(1)} %bitcast.151), custom_call_target="tpu_custom_call" | custom-call | flops 28991029248 | bytes 23068672 | tf_op jit(solution)/shard_map/pallas_call | solution.py:101
  (108 shorter events, 46.8 us)
Async XLA Ops:
  7.2 1.2 copy-start
  28.4 12.5 %all-to-all-start.1 = ((bf16[4,2,2,1,40,256]{5,4,1,3,2,0:T(8,128)(2,1)}), bf16[4,2,2,1,40,256]{5,4,1,3,2,0:T(8,128)(2,1)S(1)}, u32[]{:S(2)}, u32[]{:S(2)}) async-start(bf16[4,2,2,1,40,256]{5,4,1,3,2,0:T(8,128)(2,1)} %get-tuple-element.13), calls=%async_computation.1 | async-start | bytes 655360 | tf_op jit(solution)/shard_map/all_to_all | solution.py:150
  31.9 289.3 %all-gather.9.cloned.1.call-start = ((), (), s32[]{:S(2)}) async-start(), calls=%async_computation.5 | async-start | bytes 4718592 | tf_op jit(solution)/shard_map/all_gather | solution.py:141
  40.9 21.5 %all-to-all-start.2 = ((bf16[4,2,2,1,40,256]{5,4,1,3,2,0:T(8,128)(2,1)}), bf16[4,2,2,1,40,256]{5,4,1,3,2,0:T(8,128)(2,1)S(1)}, u32[]{:S(2)}, u32[]{:S(2)}) async-start(bf16[4,2,2,1,40,256]{5,4,1,3,2,0:T(8,128)(2,1)} %get-tuple-element.12), calls=%async_computation.2 | async-start | bytes 655360 | tf_op jit(solution)/shard_map/all_to_all | solution.py:150
  44.6 3.0 copy-start.2
  62.4 23.2 %all-to-all-start.3 = ((bf16[4,2,2,1,40,256]{5,4,1,3,2,0:T(8,128)(2,1)}), bf16[4,2,2,1,40,256]{5,4,1,3,2,0:T(8,128)(2,1)S(1)}, u32[]{:S(2)}, u32[]{:S(2)}) async-start(bf16[4,2,2,1,40,256]{5,4,1,3,2,0:T(8,128)(2,1)} %get-tuple-element.11), calls=%async_computation.3 | async-start | bytes 655360 | tf_op jit(solution)/shard_map/all_to_all | solution.py:150
  66.0 38.4 %collective-permute-start = (bf16[320,256]{1,0:T(8,128)(2,1)S(1)}, bf16[320,256]{1,0:T(8,128)(2,1)S(1)}, u32[]{:S(2)}, u32[]{:S(2)}) collective-permute-start(bf16[320,256]{1,0:T(8,128)(2,1)S(1)} %constant_dynamic-slice_fusion.8), channel_id=1, source_target_pairs={{0,1},{1,0},{2,3},{3,2},{4,5},{5,4},{6,7},{7,6},{8,9},{9,8},{10,11... | collective-permute-start | bytes 491528 | tf_op jit(solution)/shard_map/ppermute | solution.py:171
  104.6 6.2 %collective-permute-start.1 = (bf16[2,4,40,256]{3,2,1,0:T(8,128)(2,1)S(1)}, bf16[2,4,40,256]{3,2,1,0:T(8,128)(2,1)S(1)}, u32[]{:S(2)}, u32[]{:S(2)}) collective-permute-start(bf16[2,4,40,256]{3,2,1,0:T(8,128)(2,1)S(1)} %fusion.12), channel_id=1, source_target_pairs={{0,8},{8,16},{16,24},{1,9},{9,17},{17,25},{2,10},{10,18},{18,26},{... | collective-permute-start | bytes 491528 | tf_op jit(solution)/shard_map/ppermute | solution.py:183
  110.9 3.0 copy-start.3
  118.1 16.3 %collective-permute-start.2 = (bf16[320,256]{1,0:T(8,128)(2,1)S(1)}, bf16[320,256]{1,0:T(8,128)(2,1)S(1)}, u32[]{:S(2)}, u32[]{:S(2)}) collective-permute-start(bf16[320,256]{1,0:T(8,128)(2,1)S(1)} %constant_dynamic-slice_fusion.7), channel_id=1, source_target_pairs={{0,1},{1,0},{2,3},{3,2},{4,5},{5,4},{6,7},{7,6},{8,9},{9,8},{10,11... | collective-permute-start | bytes 491528 | tf_op jit(solution)/shard_map/ppermute | solution.py:171
  134.7 7.2 %collective-permute-start.3 = (bf16[2,4,40,256]{3,2,1,0:T(8,128)(2,1)S(1)}, bf16[2,4,40,256]{3,2,1,0:T(8,128)(2,1)S(1)}, u32[]{:S(2)}, u32[]{:S(2)}) collective-permute-start(bf16[2,4,40,256]{3,2,1,0:T(8,128)(2,1)S(1)} %fusion.21), channel_id=1, source_target_pairs={{0,8},{8,16},{16,24},{1,9},{9,17},{17,25},{2,10},{10,18},{18,26},{... | collective-permute-start | bytes 491528 | tf_op jit(solution)/shard_map/ppermute | solution.py:183
  146.1 16.3 %collective-permute-start.4 = (bf16[320,256]{1,0:T(8,128)(2,1)S(1)}, bf16[320,256]{1,0:T(8,128)(2,1)S(1)}, u32[]{:S(2)}, u32[]{:S(2)}) collective-permute-start(bf16[320,256]{1,0:T(8,128)(2,1)S(1)} %constant_dynamic-slice_fusion.6), channel_id=1, source_target_pairs={{0,1},{1,0},{2,3},{3,2},{4,5},{5,4},{6,7},{7,6},{8,9},{9,8},{10,11... | collective-permute-start | bytes 491528 | tf_op jit(solution)/shard_map/ppermute | solution.py:171
  162.8 7.2 %collective-permute-start.5 = (bf16[2,4,40,256]{3,2,1,0:T(8,128)(2,1)S(1)}, bf16[2,4,40,256]{3,2,1,0:T(8,128)(2,1)S(1)}, u32[]{:S(2)}, u32[]{:S(2)}) collective-permute-start(bf16[2,4,40,256]{3,2,1,0:T(8,128)(2,1)S(1)} %fusion.30), channel_id=1, source_target_pairs={{0,8},{8,16},{16,24},{1,9},{9,17},{17,25},{2,10},{10,18},{18,26},{... | collective-permute-start | bytes 491528 | tf_op jit(solution)/shard_map/ppermute | solution.py:183
  174.2 16.3 %collective-permute-start.6 = (bf16[320,256]{1,0:T(8,128)(2,1)S(1)}, bf16[320,256]{1,0:T(8,128)(2,1)S(1)}, u32[]{:S(2)}, u32[]{:S(2)}) collective-permute-start(bf16[320,256]{1,0:T(8,128)(2,1)S(1)} %constant_dynamic-slice_fusion.5), channel_id=1, source_target_pairs={{0,1},{1,0},{2,3},{3,2},{4,5},{5,4},{6,7},{7,6},{8,9},{9,8},{10,11... | collective-permute-start | bytes 491528 | tf_op jit(solution)/shard_map/ppermute | solution.py:171
  190.8 8.0 %collective-permute-start.7 = (bf16[2,4,40,256]{3,2,1,0:T(8,128)(2,1)S(1)}, bf16[2,4,40,256]{3,2,1,0:T(8,128)(2,1)S(1)}, u32[]{:S(2)}, u32[]{:S(2)}) collective-permute-start(bf16[2,4,40,256]{3,2,1,0:T(8,128)(2,1)S(1)} %fusion.39), channel_id=1, source_target_pairs={{0,8},{8,16},{16,24},{1,9},{9,17},{17,25},{2,10},{10,18},{18,26},{... | collective-permute-start | bytes 491528 | tf_op jit(solution)/shard_map/ppermute | solution.py:183
  203.0 16.4 %collective-permute-start.8 = (bf16[320,256]{1,0:T(8,128)(2,1)S(1)}, bf16[320,256]{1,0:T(8,128)(2,1)S(1)}, u32[]{:S(2)}, u32[]{:S(2)}) collective-permute-start(bf16[320,256]{1,0:T(8,128)(2,1)S(1)} %constant_dynamic-slice_fusion.4), channel_id=1, source_target_pairs={{0,1},{1,0},{2,3},{3,2},{4,5},{5,4},{6,7},{7,6},{8,9},{9,8},{10,11... | collective-permute-start | bytes 491528 | tf_op jit(solution)/shard_map/ppermute | solution.py:171
  219.6 8.1 %collective-permute-start.9 = (bf16[2,4,40,256]{3,2,1,0:T(8,128)(2,1)S(1)}, bf16[2,4,40,256]{3,2,1,0:T(8,128)(2,1)S(1)}, u32[]{:S(2)}, u32[]{:S(2)}) collective-permute-start(bf16[2,4,40,256]{3,2,1,0:T(8,128)(2,1)S(1)} %fusion.48), channel_id=1, source_target_pairs={{0,8},{8,16},{16,24},{1,9},{9,17},{17,25},{2,10},{10,18},{18,26},{... | collective-permute-start | bytes 491528 | tf_op jit(solution)/shard_map/ppermute | solution.py:183
  231.8 16.4 %collective-permute-start.10 = (bf16[320,256]{1,0:T(8,128)(2,1)S(1)}, bf16[320,256]{1,0:T(8,128)(2,1)S(1)}, u32[]{:S(2)}, u32[]{:S(2)}) collective-permute-start(bf16[320,256]{1,0:T(8,128)(2,1)S(1)} %constant_dynamic-slice_fusion.3), channel_id=1, source_target_pairs={{0,1},{1,0},{2,3},{3,2},{4,5},{5,4},{6,7},{7,6},{8,9},{9,8},{10,11... | collective-permute-start | bytes 491528 | tf_op jit(solution)/shard_map/ppermute | solution.py:171
  248.5 8.1 %collective-permute-start.11 = (bf16[2,4,40,256]{3,2,1,0:T(8,128)(2,1)S(1)}, bf16[2,4,40,256]{3,2,1,0:T(8,128)(2,1)S(1)}, u32[]{:S(2)}, u32[]{:S(2)}) collective-permute-start(bf16[2,4,40,256]{3,2,1,0:T(8,128)(2,1)S(1)} %get-tuple-element.21), channel_id=1, source_target_pairs={{0,8},{8,16},{16,24},{1,9},{9,17},{17,25},{2,10},{10,18},{18,26},{... | collective-permute-start | bytes 491528 | tf_op jit(solution)/shard_map/ppermute | solution.py:183
  260.8 41.7 %collective-permute-start.12 = (bf16[320,256]{1,0:T(8,128)(2,1)S(1)}, bf16[320,256]{1,0:T(8,128)(2,1)S(1)}, u32[]{:S(2)}, u32[]{:S(2)}) collective-permute-start(bf16[320,256]{1,0:T(8,128)(2,1)S(1)} %constant_dynamic-slice_fusion.2), channel_id=1, source_target_pairs={{0,1},{1,0},{2,3},{3,2},{4,5},{5,4},{6,7},{7,6},{8,9},{9,8},{10,11... | collective-permute-start | bytes 491528 | tf_op jit(solution)/shard_map/ppermute | solution.py:171
  303.7 16.4 %all-to-all-start.4 = ((bf16[4,8,1,32,256]{4,3,1,2,0:T(8,128)(2,1)}), bf16[4,8,1,32,256]{4,3,1,2,0:T(8,128)(2,1)S(1)}, u32[]{:S(2)}, u32[]{:S(2)}) async-start(bf16[4,8,1,32,256]{4,3,1,2,0:T(8,128)(2,1)} %copy_bitcast_fusion), calls=%async_computation.4 | async-start | bytes 1048576 | tf_op jit(solution)/shard_map/all_to_all | solution.py:194
  321.2 2.2 copy-start.4
  323.4 39.6 %copy-start.1 = (bf16[1,512,8,1,128]{4,2,3,1,0:T(8,128)(2,1)S(1)}, bf16[1,512,8,1,128]{4,2,3,1,0:T(8,128)(2,1)}, u32[]{:S(2)}) copy-start(bf16[1,512,8,1,128]{4,2,3,1,0:T(8,128)(2,1)} %param.4) | copy-start | bytes 3145732
Sparse Core Ops, SparseCore 0:
  34.3 69.0 all-gather.8
